TPU v7x, 1024 devices: a whole 8x8x8 slice. The times are simulated.
1024 devices in a mesh: dp: 16 (over z, core), expert: 64 (over y, x).
Axes of the slice: x: 8, y: 8, z: 8, core: 2. Of those that a mesh axis runs over, the one named last changes fastest.
Arguments:
- tokens: bfloat16 [8192, 3584], P('expert', 'dp'), may hold values from -6 to 6
- cotangent: bfloat16 [8192, 3584], P('expert', 'dp'), may hold values from -6 to 6
- w_in: bfloat16 [64, 3584, 1024], P('expert', 'dp'), may hold values from -0.09375 to 0.09375
- w_out: bfloat16 [64, 1024, 3584], P('expert', None, 'dp'), may hold values from -0.1875 to 0.1875
- route_token: int32 [64, 64, 8], P('expert'), may hold values from 0 to 127
- route_count: int32 [64, 64], P('expert'), may hold values from 1 to 8, as said below
- copy_plan: int32 [64], replicated, may hold values from 0 to 1, as said below
- route_prob: float32 [64, 64, 8], P('expert'), may hold values from 0.05 to 1
Outputs:
- expert_out: bfloat16 [8192, 3584], P('expert', 'dp')
- token_grad: bfloat16 [8192, 3584], P('expert', 'dp')
- w_in_grad: bfloat16 [64, 3584, 1024], P('expert', 'dp')
- w_out_grad: bfloat16 [64, 1024, 3584], P('expert', None, 'dp')
Inputs may be any that keep to these rules, and one draw needn't show every extreme that they name: `route_count`: every source routes exactly 8 rows to at least one expert, and each of the experts 0, 31, 32 and 63 receives exactly 8 rows from some source. copy_plan is 1 for experts 0, 31, 32 and 63.
All inputs are finite; a program needn't handle non-finite values.
Results may differ from a plain program's by a relative error of at most 0.0057.
Values may be sent and summed in bfloat16 or wider, within the bound.
A program may use at most 32 MiB of HBM per device.

v0:
```python
import jax
import jax.numpy as jnp
from jax import lax
from jax.sharding import PartitionSpec as P


def from_behind(x, axis, by):
    devices = lax.axis_size(axis)
    return lax.ppermute(x, axis, [(i, (i + by) % devices) for i in range(devices)])


def silu_slope(values):
    sigmoid_part = jax.nn.sigmoid(values)
    return sigmoid_part * (1.0 + values * (1.0 - sigmoid_part))


def to_hosts(buffer, half_cap, shift_by):
    return jnp.concatenate(
        [buffer[:, :half_cap], jnp.roll(buffer[:, half_cap:], shift_by, axis=0)], axis=1
    )


def on_device(tokens, cotangent, w_in, w_out, route_token, route_count, copy_plan, route_prob):
    sources = route_token.shape[1]
    capacity = route_token.shape[2]
    half_cap = capacity // 2
    half_axis = lax.axis_size("expert") // 2
    token_count = tokens.shape[0]
    slot_index = jnp.arange(capacity, dtype=jnp.int32)[None, :]
    filled = slot_index < route_count[0][:, None]
    allowed = (slot_index < half_cap) | (copy_plan[:, None] == 1)
    weights = jnp.where(filled & allowed, route_prob[0], 0.0)
    flat_token = route_token[0].reshape(-1)
    picked = jnp.take(tokens, flat_token, axis=0).reshape(sources, capacity, -1)
    cot_rows = jnp.take(cotangent, flat_token, axis=0).astype(jnp.float32)
    scaled = (weights.reshape(-1, 1) * cot_rows).astype(jnp.bfloat16).reshape(sources, capacity, -1)
    send_rows = to_hosts(picked, half_cap, half_axis)
    send_scaled = to_hosts(scaled, half_cap, half_axis)
    arrived_rows, arrived_scaled = (
        lax.all_to_all(send_rows, "expert", split_axis=0, concat_axis=0, tiled=True),
        lax.all_to_all(send_scaled, "expert", split_axis=0, concat_axis=0, tiled=True),
    )
    rows_kind = arrived_rows.reshape(sources, 2, half_cap, -1)
    scaled_kind = arrived_scaled.reshape(sources, 2, half_cap, -1)
    copy_in, copy_out = from_behind((w_in[0], w_out[0]), "expert", half_axis)
    pair_in = jnp.stack([w_in[0], copy_in])
    pair_out = jnp.stack([w_out[0], copy_out])
    pre_part = jnp.einsum("skhd,kdf->skhf", rows_kind, pair_in, preferred_element_type=jnp.float32)
    grad_part = jnp.einsum(
        "skhd,kfd->skhf", scaled_kind, pair_out, preferred_element_type=jnp.float32
    )
    pre_share, grad_share = (
        lax.psum_scatter(pre_part, "dp", scatter_dimension=3, tiled=True),
        lax.psum_scatter(grad_part, "dp", scatter_dimension=3, tiled=True),
    )
    hidden_share = jax.nn.silu(pre_share).astype(jnp.bfloat16)
    slope_share = (grad_share * silu_slope(pre_share)).astype(jnp.bfloat16)
    hidden, pre_grad = (
        lax.all_gather(hidden_share, "dp", axis=3, tiled=True),
        lax.all_gather(slope_share, "dp", axis=3, tiled=True),
    )
    expert_rows = jnp.einsum("skhf,kfd->skhd", hidden, pair_out, preferred_element_type=jnp.float32)
    input_rows = jnp.einsum("skhf,kdf->skhd", pre_grad, pair_in, preferred_element_type=jnp.float32)
    grad_in_pair = jnp.einsum(
        "skhd,skhf->kdf", rows_kind, pre_grad, preferred_element_type=jnp.float32
    )
    grad_out_pair = jnp.einsum(
        "skhf,skhd->kfd", hidden, scaled_kind, preferred_element_type=jnp.float32
    )
    back_in, back_out = from_behind((grad_in_pair[1], grad_out_pair[1]), "expert", half_axis)
    w_in_grad = (grad_in_pair[0] + back_in)[None].astype(jnp.bfloat16)
    w_out_grad = (grad_out_pair[0] + back_out)[None].astype(jnp.bfloat16)
    returned_out, returned_grad = (
        lax.all_to_all(
            expert_rows.reshape(sources, capacity, -1),
            "expert",
            split_axis=0,
            concat_axis=0,
            tiled=True,
        ),
        lax.all_to_all(
            input_rows.reshape(sources, capacity, -1),
            "expert",
            split_axis=0,
            concat_axis=0,
            tiled=True,
        ),
    )
    returned_out = to_hosts(returned_out, half_cap, -half_axis).reshape(sources * capacity, -1)
    returned_grad = to_hosts(returned_grad, half_cap, -half_axis).reshape(sources * capacity, -1)
    one_hot = (flat_token[None, :] == jnp.arange(token_count, dtype=jnp.int32)[:, None]).astype(
        jnp.float32
    )
    expert_out = jnp.dot(
        one_hot * weights.reshape(1, -1),
        returned_out,
        precision=lax.Precision.HIGHEST,
        preferred_element_type=jnp.float32,
    ).astype(jnp.bfloat16)
    token_grad = jnp.dot(
        one_hot, returned_grad, precision=lax.Precision.HIGHEST, preferred_element_type=jnp.float32
    ).astype(jnp.bfloat16)
    return (expert_out, token_grad, w_in_grad, w_out_grad)


def solution(mesh):
    in_specs = (
        P("expert", "dp"),
        P("expert", "dp"),
        P("expert", "dp", None),
        P("expert", None, "dp"),
        P("expert", None, None),
        P("expert", None),
        P(),
        P("expert", None, None),
    )
    out_specs = (
        P("expert", "dp"),
        P("expert", "dp"),
        P("expert", "dp", None),
        P("expert", None, "dp"),
    )
    return jax.shard_map(
        on_device, mesh=mesh, in_specs=in_specs, out_specs=out_specs, check_vma=False
    )
```

profile of v0, /device:TPU:1, one launch (start us, length us, event | category | flops | bytes accessed | tf_op | source)
XLA Modules:
  0.0 416.9 jit_solution(14868720870027109627)
XLA Ops:
  7.2 8.7 %collective-permute-start.1 = (bf16[224,1024]{1,0:T(8,128)(2,1)}, bf16[224,1024]{1,0:T(8,128)(2,1)S(1)}, u32[]{:S(2)}, u32[]{:S(2)}) collective-permute-start(bf16[224,1024]{1,0:T(8,128)(2,1)} %bitcast.94), channel_id=1, source_target_pairs={{0,32},{1,33},{2,34},{3,35},{4,36},{5,37},{6,38},{7,39},{8,40},{9,... | collective-permute-start | bytes 1376264 | tf_op jit(solution)/shard_map/ppermute | solution.py:9
  20.2 20.6 %all_to_all.20 = bf16[64,8,224]{2,1,0:T(8,128)(2,1)S(1)} all-to-all(bf16[64,8,224]{2,1,0:T(8,128)(2,1)S(1)} %maximum_maximum_fusion), channel_id=1, replica_groups=mesh['dp'=16,'expert'=64] {'expert'}, dimensions={0} | all-to-all | bytes 458752 | tf_op jit(solution)/shard_map/all_to_all | solution.py:40
  41.3 3.1 copy.50
  44.5 5.6 %reshape.151 = f32[1024,512]{1,0:T(8,128)} reshape(f32[1024,2,4,64]{3,2,1,0:T(4,128)} %bitcast.83) | data formatting | bytes 4194304
  51.1 3.0 collective-permute-start
  57.1 25.6 %all_to_all.21 = bf16[64,8,224]{2,1,0:T(8,128)(2,1)S(1)} all-to-all(bf16[64,8,224]{2,1,0:T(8,128)(2,1)S(1)} %maximum_maximum_fusion.1), channel_id=1, replica_groups=mesh['dp'=16,'expert'=64] {'expert'}, dimensions={0} | all-to-all | bytes 458752 | tf_op jit(solution)/shard_map/all_to_all | solution.py:41
  83.2 3.1 copy.52
  86.4 5.7 %reshape.153 = f32[1024,512]{1,0:T(8,128)} reshape(f32[1024,2,4,64]{3,2,1,0:T(4,128)} %bitcast.84) | data formatting | bytes 4194304
  92.1 35.6 %reduce-scatter.7.cloned.1.call-done = f32[64,512]{1,0:T(8,128)} async-done(((f32[1024,512]{1,0:T(8,128)}), f32[64,512]{1,0:T(8,128)}) %reduce-scatter.7.cloned.1.call-update) | async-done | bytes 131088
  128.9 65.6 %reduce-scatter.9.cloned.1.call-done = f32[64,512]{1,0:T(8,128)} async-done(((f32[1024,512]{1,0:T(8,128)}), f32[64,512]{1,0:T(8,128)}) %reduce-scatter.9.cloned.1.call-update) | async-done | bytes 131088
  197.7 46.7 %all-gather.3.cloned.1.call-done = bf16[64,2,4,1024]{0,2,1,3:T(4,128)(2,1)} async-done(((bf16[64,2,4,64]{0,2,1,3:T(4,128)(2,1)}), bf16[64,2,4,1024]{0,2,1,3:T(4,128)(2,1)}) %all-gather.3.cloned.1.call-update) | async-done | bytes 1048592 | tf_op jit(solution)/shard_map/all_gather | solution.py:59
  244.4 2.9 copy.37
  248.9 12.4 %all-to-all-start.1 = ((f32[64,8,224]{2,1,0:T(8,128)}), f32[64,8,224]{2,1,0:T(8,128)S(1)}, u32[]{:S(2)}, u32[]{:S(2)}) async-start(f32[64,8,224]{2,1,0:T(8,128)} %copy.38), calls=%async_computation.1 | async-start | bytes 1048576 | tf_op jit(solution)/shard_map/all_to_all | solution.py:74
  261.3 30.5 %all-gather.5.cloned.1.call-done = bf16[64,2,4,1024]{0,2,1,3:T(4,128)(2,1)} async-done(((bf16[64,2,4,64]{0,2,1,3:T(4,128)(2,1)}), bf16[64,2,4,1024]{0,2,1,3:T(4,128)(2,1)}) %all-gather.5.cloned.1.call-update) | async-done | bytes 1048592 | tf_op jit(solution)/shard_map/all_gather | solution.py:60
  291.8 2.9 copy.42
  294.7 2.0 fusion.4
  298.6 12.5 %all-to-all-start.3 = ((f32[64,8,224]{2,1,0:T(8,128)}), f32[64,8,224]{2,1,0:T(8,128)}, u32[]{:S(2)}, u32[]{:S(2)}) async-start(f32[64,8,224]{2,1,0:T(8,128)} %copy.43), calls=%async_computation.3 | async-start | bytes 1048576 | tf_op jit(solution)/shard_map/all_to_all | solution.py:81
  312.6 6.8 %collective-permute-start.3 = (f32[1024,224]{0,1:T(8,128)}, f32[1024,224]{0,1:T(8,128)}, u32[]{:S(2)}, u32[]{:S(2)}) collective-permute-start(f32[1024,224]{0,1:T(8,128)} %slice_bitcast_fusion), channel_id=1, source_target_pairs={{0,32},{1,33},{2,34},{3,35},{4,36},{5,37},{6,38},{7,39},{8,40},{9,... | collective-permute-start | bytes 2752520 | tf_op jit(solution)/shard_map/ppermute | solution.py:9
  322.2 2.5 collective-permute-start.2
  324.7 4.3 %all-to-all-done.3 = f32[64,8,224]{2,1,0:T(8,128)} async-done(((f32[64,8,224]{2,1,0:T(8,128)}), f32[64,8,224]{2,1,0:T(8,128)}, u32[]{:S(2)}, u32[]{:S(2)}) %all-to-all-start.3) | async-done | bytes 458784 | tf_op jit(solution)/shard_map/all_to_all | solution.py:81
  334.1 36.6 %collective-permute-done.3 = f32[1024,224]{0,1:T(8,128)} collective-permute-done((f32[1024,224]{0,1:T(8,128)}, f32[1024,224]{0,1:T(8,128)}, u32[]{:S(2)}, u32[]{:S(2)}) %collective-permute-start.3) | collective-permute-done | bytes 917536 | tf_op jit(solution)/shard_map/ppermute | solution.py:9
  370.6 2.1 fusion.15
  372.7 35.6 %collective-permute-done.2 = f32[224,1024]{1,0:T(8,128)} collective-permute-done((f32[224,1024]{1,0:T(8,128)}, f32[224,1024]{1,0:T(8,128)}, u32[]{:S(2)}, u32[]{:S(2)}) %collective-permute-start.2) | collective-permute-done | bytes 917536 | tf_op jit(solution)/shard_map/ppermute | solution.py:9
  408.3 2.1 fusion.14
  (92 shorter events, 26.3 us)
Async XLA Ops:
  7.2 120.5 %reduce-scatter.7.cloned.1.call-start = ((), (), s32[]{:S(2)}) async-start(), calls=%async_computation.8 | async-start | bytes 2228224
  7.2 33.6 %collective-permute-start.1 = (bf16[224,1024]{1,0:T(8,128)(2,1)}, bf16[224,1024]{1,0:T(8,128)(2,1)S(1)}, u32[]{:S(2)}, u32[]{:S(2)}) collective-permute-start(bf16[224,1024]{1,0:T(8,128)(2,1)} %bitcast.94), channel_id=1, source_target_pairs={{0,32},{1,33},{2,34},{3,35},{4,36},{5,37},{6,38},{7,39},{8,40},{9,... | collective-permute-start | bytes 1376264 | tf_op jit(solution)/shard_map/ppermute | solution.py:9
  19.7 21.1 %copy-start.8 = (bf16[1,224,1024]{2,1,0:T(8,128)(2,1)S(1)}, bf16[1,224,1024]{2,1,0:T(8,128)(2,1)}, u32[]{:S(2)}) copy-start(bf16[1,224,1024]{2,1,0:T(8,128)(2,1)} %param.12) | copy-start | bytes 1376260
  40.8 3.6 copy-start.9
  50.1 4.0 copy-start.15
  50.1 4.0 copy-start.14
  50.1 4.2 %copy-start.13 = (f32[1,64,8]{1,2,0:T(8,128)S(1)}, f32[1,64,8]{1,2,0:T(8,128)}, u32[]{:S(2)}) copy-start(f32[1,64,8]{1,2,0:T(8,128)} %param.17) | copy-start | bytes 6148
  50.1 4.4 %copy-start.12 = (bf16[128,224]{0,1:T(8,128)(2,1)S(1)}, bf16[128,224]{0,1:T(8,128)(2,1)}, u32[]{:S(2)}) copy-start(bf16[128,224]{0,1:T(8,128)(2,1)} %param.11) | copy-start | bytes 172036
  50.1 144.4 %reduce-scatter.9.cloned.1.call-start = ((), (), s32[]{:S(2)}) async-start(), calls=%async_computation.9 | async-start | bytes 2228224
  51.1 31.7 %collective-permute-start = (bf16[1024,224]{0,1:T(8,128)(2,1)S(1)}, bf16[1024,224]{0,1:T(8,128)(2,1)S(1)}, u32[]{:S(2)}, u32[]{:S(2)}) collective-permute-start(bf16[1024,224]{0,1:T(8,128)(2,1)S(1)} %bitcast.93), channel_id=1, source_target_pairs={{0,32},{1,33},{2,34},{3,35},{4,36},{5,37},{6,38},{7,39},{8,40},{9,... | collective-permute-start | bytes 1376264 | tf_op jit(solution)/shard_map/ppermute | solution.py:9
  82.8 3.6 copy-start.10
  92.1 152.4 %all-gather.3.cloned.1.call-start = ((), (), s32[]{:S(2)}) async-start(), calls=%async_computation.6 | async-start | bytes 2228224 | tf_op jit(solution)/shard_map/all_gather | solution.py:59
  196.7 50.7 %copy-start.7 = (bf16[1,1024,224]{1,2,0:T(8,128)(2,1)S(1)}, bf16[1,1024,224]{1,2,0:T(8,128)(2,1)}, u32[]{:S(2)}) copy-start(bf16[1,1024,224]{1,2,0:T(8,128)(2,1)} %param.13) | copy-start | bytes 1376260
  196.7 50.7 %copy-start.11 = (bf16[1024,224]{0,1:T(8,128)(2,1)S(1)}, bf16[1024,224]{0,1:T(8,128)(2,1)}, u32[]{:S(2)}) copy-start(bf16[1024,224]{0,1:T(8,128)(2,1)} %copy-done.10) | copy-start | bytes 1376260
  196.7 95.1 %all-gather.5.cloned.1.call-start = ((), (), s32[]{:S(2)}) async-start(), calls=%async_computation.7 | async-start | bytes 2228224 | tf_op jit(solution)/shard_map/all_gather | solution.py:60
  248.9 48.9 %all-to-all-start.1 = ((f32[64,8,224]{2,1,0:T(8,128)}), f32[64,8,224]{2,1,0:T(8,128)S(1)}, u32[]{:S(2)}, u32[]{:S(2)}) async-start(f32[64,8,224]{2,1,0:T(8,128)} %copy.38), calls=%async_computation.1 | async-start | bytes 1048576 | tf_op jit(solution)/shard_map/all_to_all | solution.py:74
  294.7 3.1 copy-start.2
  298.6 30.3 %all-to-all-start.3 = ((f32[64,8,224]{2,1,0:T(8,128)}), f32[64,8,224]{2,1,0:T(8,128)}, u32[]{:S(2)}, u32[]{:S(2)}) async-start(f32[64,8,224]{2,1,0:T(8,128)} %copy.43), calls=%async_computation.3 | async-start | bytes 1048576 | tf_op jit(solution)/shard_map/all_to_all | solution.py:81
  311.1 8.3 %copy-start.3 = (bf16[64,2,4,1024]{3,0,2,1:T(8,128)(2,1)S(1)}, bf16[64,2,4,1024]{3,0,2,1:T(8,128)(2,1)}, u32[]{:S(2)}) copy-start(bf16[64,2,4,1024]{3,0,2,1:T(8,128)(2,1)} %copy-done.2) | copy-start | bytes 3145732
  312.6 58.1 %collective-permute-start.3 = (f32[1024,224]{0,1:T(8,128)}, f32[1024,224]{0,1:T(8,128)}, u32[]{:S(2)}, u32[]{:S(2)}) collective-permute-start(f32[1024,224]{0,1:T(8,128)} %slice_bitcast_fusion), channel_id=1, source_target_pairs={{0,32},{1,33},{2,34},{3,35},{4,36},{5,37},{6,38},{7,39},{8,40},{9,... | collective-permute-start | bytes 2752520 | tf_op jit(solution)/shard_map/ppermute | solution.py:9
  321.1 11.2 %copy-start.5 = (f32[64,8,224]{2,1,0:T(8,128)S(1)}, f32[64,8,224]{2,1,0:T(8,128)}, u32[]{:S(2)}) copy-start(f32[64,8,224]{2,1,0:T(8,128)} %copy-done.4) | copy-start | bytes 1376260
  322.2 10.2 %slice-start = ((f32[64,8,224]{2,1,0:T(8,128)}), f32[64,4,224]{2,1,0:T(4,128)S(1)}, s32[]{:S(2)}) async-start(f32[64,8,224]{2,1,0:T(8,128)} %copy-done.4), calls=%async_computation.10 | async-start | bytes 524288 | tf_op jit(solution)/shard_map/slice | solution.py:19
  322.2 86.1 %collective-permute-start.2 = (f32[224,1024]{1,0:T(8,128)}, f32[224,1024]{1,0:T(8,128)}, u32[]{:S(2)}, u32[]{:S(2)}) collective-permute-start(f32[224,1024]{1,0:T(8,128)} %slice_bitcast_fusion.2), channel_id=1, source_target_pairs={{0,32},{1,33},{2,34},{3,35},{4,36},{5,37},{6,38},{7,39},{8,40},{9,... | collective-permute-start | bytes 2752520 | tf_op jit(solution)/shard_map/ppermute | solution.py:9
  332.3 76.0 %copy-start.1 = (f32[2,224,1024]{2,1,0:T(8,128)S(1)}, f32[2,224,1024]{2,1,0:T(8,128)}, u32[]{:S(2)}) copy-start(f32[2,224,1024]{2,1,0:T(8,128)} %copy-done) | copy-start | bytes 5505028
  (3 other events, 3.1 us)
Sparse Core Ops, SparseCore 0:
  50.2 77.3 reduce-scatter.6
  131.1 63.3 reduce-scatter.8
  197.2 47.1 all-gather.2
  247.0 44.7 all-gather.4
where the time goes:
time: 419 us; the launch traced here: 417 us
  waiting for transfers between devices  255 us (61%)
  starting transfers between devices  46.2 us (11%)
  blocking collectives  46.2 us (11%)
  local copies, waits for them, and re-layouts  43.2 us (10%)
  between operations  14.2 us (3%)
  matrix products  7.13 us (2%)
  other arithmetic  5.01 us (1%)
    unnamed x6, waiting for transfers between devices  101 us
    ppermute x4, waiting for transfers between devices, from_behind(): lax.ppermute(x, axis, [(i, (i + by) % devices) for i in range(devices)])  72.2 us
    all_gather x1, waiting for transfers between devices, on_device(): lax.all_gather(hidden_share, 'dp', axis=3, tiled=True)  46.7 us
    all_gather x1, waiting for transfers between devices, on_device(): lax.all_gather(slope_share, 'dp', axis=3, tiled=True)  30.5 us
    all_to_all x1, blocking collectives, on_device(): lax.all_to_all(send_scaled, 'expert', split_axis=0, concat_axis=0, tiled=...  25.6 us
    unnamed x44, local copies, waits for them, and re-layouts  24.8 us
    ppermute x4, starting transfers between devices, from_behind(): lax.ppermute(x, axis, [(i, (i + by) % devices) for i in range(devices)])  21 us
    all_to_all x1, blocking collectives, on_device(): lax.all_to_all(send_rows, 'expert', split_axis=0, concat_axis=0, tiled=True)  20.6 us
  transfers between devices with their start and end apart: 10, of which 7 were waited for; matrix products, arithmetic and copies ran while one was open for 9% of the time, Pallas kernels for 0%

commit v1 on v0

v1 whole, which is shorter than its diff:
```python
import functools
import math

import jax
import jax.numpy as jnp
from jax import lax
from jax.experimental import pallas as pl
from jax.experimental.pallas import tpu as pltpu
from jax.sharding import PartitionSpec as P

F32 = jnp.float32
BF16 = jnp.bfloat16
MESH = pl.DeviceIdType.MESH
CHUNKS = 4
SKEW = 1


def dot(a, b, ca, cb, precision=None):
    return lax.dot_general(
        a, b, (((ca,), (cb,)), ((), ())), precision=precision, preferred_element_type=F32
    )


def iota(shape, axis):
    return lax.broadcasted_iota(jnp.int32, shape, axis)


def moe_kernel(
    experts,
    zs,
    tok_ref,
    cot_ref,
    w_in_ref,
    w_out_ref,
    route_ref,
    count_ref,
    plan_ref,
    prob_ref,
    out_ref,
    tgrad_ref,
    gin_ref,
    gout_ref,
    send_buf,
    recv_buf,
    rows_buf,
    scaled_buf,
    pair_send,
    pair_recv,
    part_buf,
    rs_send,
    rs_recv,
    act_buf,
    ret_send,
    ret_recv,
    comb_buf,
    a2a_send_sem,
    a2a_recv_sem,
    pair_send_sem,
    pair_recv_sem,
    rs_send_sem,
    rs_recv_sem,
    ag_send_sem,
    ag_recv_sem,
    sib_send_sem,
    sib_recv_sem,
    ret_send_sem,
    ret_recv_sem,
):
    cap = route_ref.shape[0]
    half_cap = cap // 2
    width, tokens = tok_ref.shape
    hidden = w_in_ref.shape[1]
    half = hidden // 2
    slots = experts * cap
    chunk_rows = slots // CHUNKS
    chunk_blocks = experts // CHUNKS
    own_rows = chunk_rows // zs
    far, near = zs // 2, zs - 1 - zs // 2
    nx = math.isqrt(experts)
    ny = experts // nx

    me = lax.axis_index("expert")
    my_y, my_x = me // nx, me % nx
    dp = lax.axis_index("dp")
    z, core = dp // 2, dp % 2
    other = 1 - core
    sibling = {"dp": z * 2 + other}
    turn = 1 - 2 * core
    ahead = {"dp": ((z + turn + zs) % zs) * 2 + core}
    behind = {"dp": ((z - turn + zs) % zs) * 2 + core}

    def offset(j):
        return (3 * (j // nx)) % ny, j % nx

    def to_expert(j):
        dy, dx = offset(j)
        return ((my_y + dy) % ny) * nx + (my_x + dx) % nx

    def from_expert(j):
        dy, dx = offset(j)
        return ((my_y - dy + ny) % ny) * nx + (my_x - dx + nx) % nx

    def owner(steps):
        return (z + turn * steps + 2 * zs) % zs

    def remote(src, dst, send_sem, recv_sem, device):
        return pltpu.make_async_remote_copy(
            src_ref=src,
            dst_ref=dst,
            send_sem=send_sem,
            recv_sem=recv_sem,
            device_id=device,
            device_id_type=MESH,
        )

    barrier = pltpu.get_barrier_semaphore()

    def greet(j, carry):
        pl.semaphore_signal(
            barrier, inc=1, device_id={"expert": to_expert(j)}, device_id_type=MESH
        )
        return carry

    lax.fori_loop(1, experts, greet, 0)
    for device in (sibling, ahead, behind):
        pl.semaphore_signal(barrier, inc=1, device_id=device, device_id_type=MESH)

    slot = iota((cap, experts), 0)
    used = (slot < count_ref[...]) & ((slot < half_cap) | (plan_ref[...] == 1))
    weights = jnp.where(used, prob_ref[...], 0.0)
    spread = (iota((slots, experts), 0) // cap == iota((slots, experts), 1)).astype(F32)
    mine = iota((slots, cap), 0) % cap == iota((slots, cap), 1)

    def as_column(table):
        wide = dot(spread, table, 1, 1, lax.Precision.HIGHEST)
        return jnp.sum(jnp.where(mine, wide, 0.0), axis=1, keepdims=True)

    token_col = as_column(route_ref[...].astype(F32))
    weight_col = as_column(weights)
    hot = (token_col == iota((slots, tokens), 1).astype(F32)).astype(F32)
    hot16 = hot.astype(BF16)
    picked = dot(hot16, tok_ref[...], 1, 1).reshape(experts, cap, width)
    scaled = (weight_col * dot(hot16, cot_ref[...], 1, 1)).reshape(experts, cap, width)
    send_buf[...] = jnp.concatenate([picked, scaled], axis=1).astype(BF16)

    pl.semaphore_wait(barrier, experts - 1 + 3)

    def dispatch(j, carry):
        e = to_expert(j)
        remote(
            send_buf.at[e],
            recv_buf.at[j],
            a2a_send_sem,
            a2a_recv_sem.at[j // chunk_blocks],
            {"expert": e},
        ).start()
        return carry

    lax.fori_loop(1, experts, dispatch, 0)
    recv_buf[0] = send_buf[me]

    weighted = (hot * weight_col).T
    weighted_hi = weighted.astype(BF16)
    comb_buf[0] = weighted_hi
    comb_buf[1] = (weighted - weighted_hi.astype(F32)).astype(BF16)
    comb_buf[2] = hot.T.astype(BF16)

    def chunk_slice(k):
        return pl.ds(k * chunk_rows, chunk_rows)

    def share_rows(k, steps):
        start = pl.multiple_of(k * chunk_rows + owner(steps) * own_rows, own_rows)
        return pl.ds(start, own_rows)

    def part_of(k, steps):
        start = pl.multiple_of(owner(steps) * own_rows, own_rows)
        return part_buf[k, :, pl.ds(start, own_rows), :]

    def pair_copy(k):
        return remote(
            pair_send.at[k],
            pair_recv.at[k],
            pair_send_sem.at[k],
            pair_recv_sem.at[k],
            sibling,
        )

    def rs_copy(k, n):
        return remote(
            rs_send.at[k, n],
            rs_recv.at[k, n],
            rs_send_sem.at[k, n],
            rs_recv_sem.at[k, n],
            ahead if n < far else behind,
        )

    def ag_copy(k, n):
        s = -n if n < far else n - far
        place = act_buf.at[core, :, share_rows(k, s), :]
        return remote(
            place,
            place,
            ag_send_sem.at[k, n],
            ag_recv_sem.at[k, n],
            ahead if n < far else behind,
        )

    def sib_copy(k, steps, n):
        place = act_buf.at[core, :, share_rows(k, steps), :]
        return remote(place, place, sib_send_sem.at[k, n], sib_recv_sem.at[k], sibling)

    def partials(k):
        first = 1 if k == 0 else 0
        blocks = recv_buf.at[pl.ds(k * chunk_blocks + first, chunk_blocks - first)]
        remote(blocks, blocks, a2a_send_sem, a2a_recv_sem.at[k], sibling).wait_recv()
        both = recv_buf[pl.ds(k * chunk_blocks, chunk_blocks)].astype(F32)
        rows = both[:, :cap].reshape(chunk_rows, width).astype(BF16)
        grads = both[:, cap:].reshape(chunk_rows, width).astype(BF16)
        rows_buf[chunk_slice(k), :] = rows
        scaled_buf[chunk_slice(k), :] = grads
        pre = dot(rows, w_in_ref[...], 1, 0)
        grad = dot(grads, w_out_ref[...], 1, 0)
        low = core == 0
        part_buf[k, 0] = jnp.where(low, pre[:, :half], pre[:, half:])
        part_buf[k, 1] = jnp.where(low, grad[:, :half], grad[:, half:])
        pair_send[k, 0] = jnp.where(low, pre[:, half:], pre[:, :half]).astype(BF16)
        pair_send[k, 1] = jnp.where(low, grad[:, half:], grad[:, :half]).astype(BF16)
        pair_copy(k).start()

    def rs_start(k):
        pair_copy(k).wait_recv()
        part_buf[k] = part_buf[k] + pair_recv[k].astype(F32)
        rs_send[k, 0] = part_of(k, far).astype(BF16)
        rs_copy(k, 0).start()
        rs_send[k, far] = part_of(k, -near).astype(BF16)
        rs_copy(k, far).start()

    def rs_step(k, s):
        for base, length, sign in ((0, far, 1), (far, near, -1)):
            if s < length:
                n = base + s
                rs_copy(k, n - 1).wait_recv()
                mixed = part_of(k, sign * (length - s)) + rs_recv[k, n - 1].astype(F32)
                rs_send[k, n] = mixed.astype(BF16)
                rs_copy(k, n).start()

    def activate(k):
        rs_copy(k, far - 1).wait_recv()
        total = part_of(k, 0) + rs_recv[k, far - 1].astype(F32)
        rs_copy(k, far + near - 1).wait_recv()
        total = total + rs_recv[k, far + near - 1].astype(F32)
        pre, grad = total[0], total[1]
        gate = 1.0 / (1.0 + jnp.exp(-pre))
        act_buf[core, 0, share_rows(k, 0), :] = (pre * gate).astype(BF16)
        slope = gate * (1.0 + pre * (1.0 - gate))
        act_buf[core, 1, share_rows(k, 0), :] = (grad * slope).astype(BF16)
        ag_copy(k, 0).start()
        ag_copy(k, far).start()
        sib_copy(k, 0, 0).start()

    def ag_step(k, s):
        for base, length, sign in ((0, far, -1), (far, near, 1)):
            if s <= length:
                ag_came(k, base + s - 1, sign * s)
                if s < length:
                    ag_copy(k, base + s).start()
                sib_copy(k, sign * s, base + s if base == 0 else far + s).start()

    def ag_came(k, n, steps):
        place = act_buf.at[core, :, share_rows(k, steps), :]
        remote(place, place, ag_send_sem.at[k, n], ag_recv_sem.at[k, n], sibling).wait_recv()

    def returns(k):
        place = act_buf.at[other, :, chunk_slice(k), :]
        remote(place, place, sib_send_sem.at[k, 0], sib_recv_sem.at[k], sibling).wait_recv()
        rows = chunk_slice(k)
        out_rows = dot(act_buf[0, 0, rows, :], w_out_ref[:, :half], 1, 1)
        out_rows = out_rows + dot(act_buf[1, 0, rows, :], w_out_ref[:, half:], 1, 1)
        in_rows = dot(act_buf[0, 1, rows, :], w_in_ref[:, :half], 1, 1)
        in_rows = in_rows + dot(act_buf[1, 1, rows, :], w_in_ref[:, half:], 1, 1)
        ret_send[pl.ds(k * chunk_blocks, chunk_blocks)] = jnp.concatenate(
            [
                out_rows.reshape(chunk_blocks, cap, width),
                in_rows.reshape(chunk_blocks, cap, width),
            ],
            axis=1,
        ).astype(BF16)
        if k == 0:
            ret_recv[me] = ret_send[0]

        def give_back(j, carry):
            remote(
                ret_send.at[j],
                ret_recv.at[me],
                ret_send_sem,
                ret_recv_sem,
                {"expert": from_expert(j)},
            ).start()
            return carry

        first = 1 if k == 0 else 0
        lax.fori_loop(k * chunk_blocks + first, (k + 1) * chunk_blocks, give_back, 0)

    stages = [partials, rs_start]
    for s in range(1, far):
        stages.append(functools.partial(lambda k, s: rs_step(k, s), s=s))
    stages.append(activate)
    for s in range(1, far + 1):
        stages.append(functools.partial(lambda k, s: ag_step(k, s), s=s))
    stages.append(returns)
    for t in range(len(stages) + SKEW * (CHUNKS - 1)):
        for k in range(CHUNKS):
            if 0 <= t - SKEW * k < len(stages):
                stages[t - SKEW * k](k)

    for h in range(2):
        cols = pl.ds(h * half, half)
        gin_ref[:, cols] = dot(rows_buf[...], act_buf[h, 1], 0, 0).astype(BF16)
        gout_ref[:, cols] = dot(scaled_buf[...], act_buf[h, 0], 0, 0).astype(BF16)

    blocks = ret_recv.at[pl.ds(0, experts - 1)]
    remote(blocks, blocks, ret_send_sem, ret_recv_sem, sibling).wait_recv()
    both = ret_recv[...].astype(F32)
    out_rows = both[:, :cap].reshape(slots, width).astype(BF16)
    in_rows = both[:, cap:].reshape(slots, width).astype(BF16)
    sums = dot(comb_buf[0], out_rows, 1, 0) + dot(comb_buf[1], out_rows, 1, 0)
    out_ref[...] = sums.T.astype(BF16)
    tgrad_ref[...] = dot(comb_buf[2], in_rows, 1, 0).T.astype(BF16)

    blocks = send_buf.at[pl.ds(0, experts - 1)]
    remote(blocks, blocks, a2a_send_sem, a2a_recv_sem.at[0], sibling).wait_send()
    blocks = ret_send.at[pl.ds(1, experts - 1)]
    remote(blocks, blocks, ret_send_sem, ret_recv_sem, sibling).wait_send()
    for k in range(CHUNKS):
        pair_copy(k).wait_send()
        for n in range(far + near):
            rs_copy(k, n).wait_send()
            ag_copy(k, n).wait_send()
        for n in range(zs):
            sib_copy(k, 0, n).wait_send()


def on_device(tokens, cotangent, w_in, w_out, route_token, route_count, copy_plan, route_prob):
    experts, cap = route_token.shape[1:]
    zs = lax.axis_size("dp") // 2
    count, width = tokens.shape
    hidden = w_in.shape[2]
    half = hidden // 2
    slots = experts * cap
    chunk_rows = slots // CHUNKS
    own_rows = chunk_rows // zs
    vmem = pl.BlockSpec(memory_space=pltpu.VMEM)
    dma = pltpu.SemaphoreType.DMA
    out, tgrad, gin, gout = pl.pallas_call(
        functools.partial(moe_kernel, experts, zs),
        out_shape=(
            jax.ShapeDtypeStruct((width, count), BF16),
            jax.ShapeDtypeStruct((width, count), BF16),
            jax.ShapeDtypeStruct((width, hidden), BF16),
            jax.ShapeDtypeStruct((width, hidden), BF16),
        ),
        in_specs=[vmem] * 8,
        out_specs=(vmem,) * 4,
        scratch_shapes=[
            pltpu.VMEM((experts, 2 * cap, width), BF16),
            pltpu.VMEM((experts, 2 * cap, width), BF16),
            pltpu.VMEM((slots, width), BF16),
            pltpu.VMEM((slots, width), BF16),
            pltpu.VMEM((CHUNKS, 2, chunk_rows, half), BF16),
            pltpu.VMEM((CHUNKS, 2, chunk_rows, half), BF16),
            pltpu.VMEM((CHUNKS, 2, chunk_rows, half), F32),
            pltpu.VMEM((CHUNKS, zs - 1, 2, own_rows, half), BF16),
            pltpu.VMEM((CHUNKS, zs - 1, 2, own_rows, half), BF16),
            pltpu.VMEM((2, 2, slots, half), BF16),
            pltpu.VMEM((experts, 2 * cap, width), BF16),
            pltpu.VMEM((experts, 2 * cap, width), BF16),
            pltpu.VMEM((3, count, slots), BF16),
            dma,
            dma((CHUNKS,)),
            dma((CHUNKS,)),
            dma((CHUNKS,)),
            dma((CHUNKS, zs - 1)),
            dma((CHUNKS, zs - 1)),
            dma((CHUNKS, zs - 1)),
            dma((CHUNKS, zs - 1)),
            dma((CHUNKS, zs)),
            dma((CHUNKS,)),
            dma,
            dma,
        ],
        compiler_params=pltpu.CompilerParams(
            collective_id=0, has_side_effects=True, vmem_limit_bytes=40 << 20
        ),
        name="moe_layer",
    )(
        tokens.T,
        cotangent.T,
        w_in[0],
        w_out[0].T,
        route_token[0].T,
        route_count,
        copy_plan[None],
        route_prob[0].T,
    )
    return out.T, tgrad.T, gin[None], gout.T[None]


def solution(mesh):
    in_specs = (
        P("expert", "dp"),
        P("expert", "dp"),
        P("expert", "dp", None),
        P("expert", None, "dp"),
        P("expert", None, None),
        P("expert", None),
        P(),
        P("expert", None, None),
    )
    out_specs = (
        P("expert", "dp"),
        P("expert", "dp"),
        P("expert", "dp", None),
        P("expert", None, "dp"),
    )
    return jax.shard_map(
        on_device, mesh=mesh, in_specs=in_specs, out_specs=out_specs, check_vma=False
    )
```

time: 419 us -> 96.3 us (0.23)
  waiting for transfers between devices: 255 us -> 0 us
  Pallas kernels: 0 us -> 88.1 us
  blocking collectives: 46.2 us -> 0 us
  starting transfers between devices: 46.2 us -> 0 us
  local copies, waits for them, and re-layouts: 43.2 us -> 7.13 us
  between operations: 14.2 us -> 0.68 us
  matrix products: 7.13 us -> 0 us
  other arithmetic: 5.01 us -> 0 us
    unnamed x6 -> x0, waiting for transfers between devices: 101 us -> none
    pallas_call x0 -> x1, Pallas kernels: none -> 88.1 us  [on_device(): pl.pallas_call(functools.partial(moe_kernel, experts, zs), out_shape=(jax...]
    all_gather x2 -> x0, waiting for transfers between devices: 77.1 us -> none  [the longest x1 46.7 us: on_device(): lax.all_gather(hidden_share, 'dp', axis=3, tiled=True)]
    ppermute x4 -> x0, waiting for transfers between devices: 72.2 us -> none  [from_behind(): lax.ppermute(x, axis, [(i, (i + by) % devices) for i in range(devices)])]
    all_to_all x2 -> x0, blocking collectives: 46.2 us -> none  [the longest x1 25.6 us: on_device(): lax.all_to_all(send_scaled, 'expert', split_axis=0, concat_axis=0, tiled=...]
    all_to_all x2 -> x0, starting transfers between devices: 24.9 us -> none  [the longest x1 12.5 us: on_device(): lax.all_to_all(input_rows.reshape(sources, capacity, -1), 'expert', split...]
    ppermute x4 -> x0, starting transfers between devices: 21 us -> none  [from_behind(): lax.ppermute(x, axis, [(i, (i + by) % devices) for i in range(devices)])]
    unnamed x44 -> x20, local copies, waits for them, and re-layouts: 24.8 us -> 7.13 us
  transfers between devices with their start and end apart: 10 -> 0, of which waited for: 7 -> 0; matrix products, arithmetic and copies ran while one was open for 9% -> 0% of each run, Pallas kernels for 0% -> 0%
where the time goes in v1:
time: 96.3 us; the launch traced here: 95.9 us
  Pallas kernels  88.1 us (91%)
  local copies, waits for them, and re-layouts  7.13 us (7%)
    pallas_call x1, Pallas kernels, on_device(): pl.pallas_call(functools.partial(moe_kernel, experts, zs), out_shape=(jax...  88.1 us
    unnamed x20, local copies, waits for them, and re-layouts  7.13 us

profile of v1, /device:TPU:1, one launch (start us, length us, event | category | flops | bytes accessed | tf_op | source)
XLA Modules:
  0.0 95.9 jit_solution(5150536507764375803)
XLA Ops:
  0.6 0.0 copy-start.5
  0.6 0.0 copy-start.4
  0.7 0.0 copy-start.6
  0.7 0.0 copy-start.7
  0.7 0.6 copy-done.5
  1.3 0.0 copy-done.4
  1.3 0.0 copy-done.6
  1.3 0.0 copy-done.7
  1.3 0.0 copy-start
  1.3 1.0 %copy-done = bf16[1,224,1024]{2,1,0:T(8,128)(2,1)S(1)} copy-done((bf16[1,224,1024]{2,1,0:T(8,128)(2,1)S(1)}, bf16[1,224,1024]{2,1,0:T(8,128)(2,1)}, u32[]{:S(2)}) %copy-start) | copy-done | bytes 458776
  2.4 0.0 copy-start.1
  2.4 1.0 %copy-done.1 = bf16[1,1024,224]{1,2,0:T(8,128)(2,1)S(1)} copy-done((bf16[1,1024,224]{1,2,0:T(8,128)(2,1)S(1)}, bf16[1,1024,224]{1,2,0:T(8,128)(2,1)}, u32[]{:S(2)}) %copy-start.1) | copy-done | bytes 458776
  3.4 0.0 copy-start.2
  3.4 0.8 copy-done.2
  4.2 0.0 copy-start.3
  4.2 0.8 copy-done.3
  5.0 88.1 %moe_layer.1 = (bf16[224,128]{1,0:T(8,128)(2,1)S(1)}, bf16[224,128]{1,0:T(8,128)(2,1)S(1)}, bf16[224,1024]{1,0:T(8,128)(2,1)S(1)}, bf16[224,1024]{1,0:T(8,128)(2,1)S(1)}) custom-call(bf16[224,128]{1,0:T(8,128)(2,1)S(1)} %bitcast.25, bf16[224,128]{1,0:T(8,128)(2,1)S(1)} %bitcast.26, bf16[224,1024]{1,0:T(8,128)(2,1)S(1)} %bitcast.19, ...), custom_call_target="tpu_custom_call" | custom-call | tf_op jit(solution)/shard_map/moe_layer/pallas_call | solution.py:354
  93.1 0.6 copy.16
  93.7 0.6 copy.17
  94.4 0.8 copy.18
  95.1 0.8 copy.19
Async XLA Ops:
  0.6 0.7 copy-start.5
  0.6 0.7 copy-start.4
  0.7 0.7 copy-start.6
  0.7 0.7 copy-start.7
  1.3 1.0 %copy-start = (bf16[1,224,1024]{2,1,0:T(8,128)(2,1)S(1)}, bf16[1,224,1024]{2,1,0:T(8,128)(2,1)}, u32[]{:S(2)}) copy-start(bf16[1,224,1024]{2,1,0:T(8,128)(2,1)} %param.10) | copy-start | bytes 1376260
  2.4 1.0 %copy-start.1 = (bf16[1,1024,224]{1,2,0:T(8,128)(2,1)S(1)}, bf16[1,1024,224]{1,2,0:T(8,128)(2,1)}, u32[]{:S(2)}) copy-start(bf16[1,1024,224]{1,2,0:T(8,128)(2,1)} %param.11) | copy-start | bytes 1376260
  3.4 0.8 copy-start.2
  4.2 0.8 copy-start.3

commit v2 on v1

--- a/solution.py
+++ b/solution.py
@@ -12,7 +12,8 @@
 BF16 = jnp.bfloat16
 MESH = pl.DeviceIdType.MESH
 CHUNKS = 4
-SKEW = 1
+STARTS = (0, 1, 2, 3)
+FLIGHT = 4
 
 
 def dot(a, b, ca, cb, precision=None):
@@ -25,9 +26,31 @@
     return lax.broadcasted_iota(jnp.int32, shape, axis)
 
 
+def offsets(ny, nx):
+    def hops(o):
+        return min(o[0], ny - o[0]) + min(o[1], nx - o[1])
+
+    near = sorted(((dy, dx) for dy in range(ny) for dx in range(nx)), key=hops)
+    size = len(near) // CHUNKS
+    return near[:size] + near[2 * size :] + near[size : 2 * size] if CHUNKS > 1 else near
+
+
 def moe_kernel(
     experts,
     zs,
+    tok_hbm,
+    cot_hbm,
+    w_in_hbm,
+    w_out_hbm,
+    route_hbm,
+    count_hbm,
+    plan_hbm,
+    prob_hbm,
+    offset_hbm,
+    out_hbm,
+    tgrad_hbm,
+    gin_hbm,
+    gout_hbm,
     tok_ref,
     cot_ref,
     w_in_ref,
@@ -36,10 +59,7 @@
     count_ref,
     plan_ref,
     prob_ref,
-    out_ref,
-    tgrad_ref,
-    gin_ref,
-    gout_ref,
+    offset_ref,
     send_buf,
     recv_buf,
     rows_buf,
@@ -53,6 +73,13 @@
     ret_send,
     ret_recv,
     comb_buf,
+    sums_buf,
+    out_ref,
+    tgrad_ref,
+    gin_ref,
+    gout_ref,
+    load_sem,
+    store_sem,
     a2a_send_sem,
     a2a_recv_sem,
     pair_send_sem,
@@ -89,15 +116,14 @@
     ahead = {"dp": ((z + turn + zs) % zs) * 2 + core}
     behind = {"dp": ((z - turn + zs) % zs) * 2 + core}
 
-    def offset(j):
-        return (3 * (j // nx)) % ny, j % nx
+    places = offsets(ny, nx)
 
     def to_expert(j):
-        dy, dx = offset(j)
+        dy, dx = places[j]
         return ((my_y + dy) % ny) * nx + (my_x + dx) % nx
 
     def from_expert(j):
-        dy, dx = offset(j)
+        dy, dx = places[j]
         return ((my_y - dy + ny) % ny) * nx + (my_x - dx + nx) % nx
 
     def owner(steps):
@@ -113,25 +139,47 @@
             device_id_type=MESH,
         )
 
+    pairs = (
+        (route_hbm, route_ref),
+        (count_hbm, count_ref),
+        (plan_hbm, plan_ref),
+        (prob_hbm, prob_ref),
+        (offset_hbm, offset_ref),
+        (tok_hbm, tok_ref),
+        (cot_hbm, cot_ref),
+        (w_in_hbm, w_in_ref),
+        (w_out_hbm, w_out_ref),
+    )
+    loads = [pltpu.make_async_copy(a, b, load_sem.at[i]) for i, (a, b) in enumerate(pairs)]
+    for load in loads:
+        load.start()
+
     barrier = pltpu.get_barrier_semaphore()
 
-    def greet(j, carry):
+    def distance(j):
+        dy, dx = places[j]
+        return min(dy, ny - dy) + min(dx, nx - dx)
+
+    for j in sorted(range(1, experts), key=distance, reverse=True):
         pl.semaphore_signal(
             barrier, inc=1, device_id={"expert": to_expert(j)}, device_id_type=MESH
         )
-        return carry
-
-    lax.fori_loop(1, experts, greet, 0)
     for device in (sibling, ahead, behind):
         pl.semaphore_signal(barrier, inc=1, device_id=device, device_id_type=MESH)
 
+    for load in loads[:5]:
+        load.wait()
     slot = iota((cap, experts), 0)
     used = (slot < count_ref[...]) & ((slot < half_cap) | (plan_ref[...] == 1))
     weights = jnp.where(used, prob_ref[...], 0.0)
     spread = (iota((slots, experts), 0) // cap == iota((slots, experts), 1)).astype(F32)
+    there_y = (offset_ref[0:1, :] + my_y) % ny
+    there_x = (offset_ref[1:2, :] + my_x) % nx
+    order = (iota((experts, experts), 0) == there_y * nx + there_x).astype(F32)
     mine = iota((slots, cap), 0) % cap == iota((slots, cap), 1)
 
     def as_column(table):
+        table = dot(table, order, 1, 0, lax.Precision.HIGHEST)
         wide = dot(spread, table, 1, 1, lax.Precision.HIGHEST)
         return jnp.sum(jnp.where(mine, wide, 0.0), axis=1, keepdims=True)
 
@@ -139,31 +187,35 @@
     weight_col = as_column(weights)
     hot = (token_col == iota((slots, tokens), 1).astype(F32)).astype(F32)
     hot16 = hot.astype(BF16)
+    for load in loads[5:7]:
+        load.wait()
     picked = dot(hot16, tok_ref[...], 1, 1).reshape(experts, cap, width)
     scaled = (weight_col * dot(hot16, cot_ref[...], 1, 1)).reshape(experts, cap, width)
     send_buf[...] = jnp.concatenate([picked, scaled], axis=1).astype(BF16)
 
     pl.semaphore_wait(barrier, experts - 1 + 3)
 
-    def dispatch(j, carry):
-        e = to_expert(j)
-        remote(
-            send_buf.at[e],
-            recv_buf.at[j],
-            a2a_send_sem,
-            a2a_recv_sem.at[j // chunk_blocks],
-            {"expert": e},
-        ).start()
-        return carry
-
-    lax.fori_loop(1, experts, dispatch, 0)
-    recv_buf[0] = send_buf[me]
+    def dispatch_chunk(k):
+        for j in range(max(1, k * chunk_blocks), (k + 1) * chunk_blocks):
+            remote(
+                send_buf.at[j],
+                recv_buf.at[j],
+                a2a_send_sem,
+                a2a_recv_sem.at[k],
+                {"expert": to_expert(j)},
+            ).start()
+
+    for k in range(FLIGHT):
+        dispatch_chunk(k)
+    recv_buf[0] = send_buf[0]
 
     weighted = (hot * weight_col).T
     weighted_hi = weighted.astype(BF16)
     comb_buf[0] = weighted_hi
     comb_buf[1] = (weighted - weighted_hi.astype(F32)).astype(BF16)
     comb_buf[2] = hot.T.astype(BF16)
+    for load in loads[7:]:
+        load.wait()
 
     def chunk_slice(k):
         return pl.ds(k * chunk_rows, chunk_rows)
@@ -213,6 +265,8 @@
         first = 1 if k == 0 else 0
         blocks = recv_buf.at[pl.ds(k * chunk_blocks + first, chunk_blocks - first)]
         remote(blocks, blocks, a2a_send_sem, a2a_recv_sem.at[k], sibling).wait_recv()
+        if k + FLIGHT < CHUNKS:
+            dispatch_chunk(k + FLIGHT)
         both = recv_buf[pl.ds(k * chunk_blocks, chunk_blocks)].astype(F32)
         rows = both[:, :cap].reshape(chunk_rows, width).astype(BF16)
         grads = both[:, cap:].reshape(chunk_rows, width).astype(BF16)
@@ -286,20 +340,16 @@
             axis=1,
         ).astype(BF16)
         if k == 0:
-            ret_recv[me] = ret_send[0]
-
-        def give_back(j, carry):
+            ret_recv[0] = ret_send[0]
+
+        for j in range(max(1, k * chunk_blocks), (k + 1) * chunk_blocks):
             remote(
                 ret_send.at[j],
-                ret_recv.at[me],
+                ret_recv.at[j],
                 ret_send_sem,
-                ret_recv_sem,
+                ret_recv_sem.at[k],
                 {"expert": from_expert(j)},
             ).start()
-            return carry
-
-        first = 1 if k == 0 else 0
-        lax.fori_loop(k * chunk_blocks + first, (k + 1) * chunk_blocks, give_back, 0)
 
     stages = [partials, rs_start]
     for s in range(1, far):
@@ -308,29 +358,47 @@
     for s in range(1, far + 1):
         stages.append(functools.partial(lambda k, s: ag_step(k, s), s=s))
     stages.append(returns)
-    for t in range(len(stages) + SKEW * (CHUNKS - 1)):
-        for k in range(CHUNKS):
-            if 0 <= t - SKEW * k < len(stages):
-                stages[t - SKEW * k](k)
+    steps = [(n + STARTS[k], k, n) for k in range(CHUNKS) for n in range(len(stages))]
+    for _, k, n in sorted(steps):
+        stages[n](k)
 
     for h in range(2):
         cols = pl.ds(h * half, half)
         gin_ref[:, cols] = dot(rows_buf[...], act_buf[h, 1], 0, 0).astype(BF16)
         gout_ref[:, cols] = dot(scaled_buf[...], act_buf[h, 0], 0, 0).astype(BF16)
 
-    blocks = ret_recv.at[pl.ds(0, experts - 1)]
-    remote(blocks, blocks, ret_send_sem, ret_recv_sem, sibling).wait_recv()
-    both = ret_recv[...].astype(F32)
-    out_rows = both[:, :cap].reshape(slots, width).astype(BF16)
-    in_rows = both[:, cap:].reshape(slots, width).astype(BF16)
-    sums = dot(comb_buf[0], out_rows, 1, 0) + dot(comb_buf[1], out_rows, 1, 0)
-    out_ref[...] = sums.T.astype(BF16)
-    tgrad_ref[...] = dot(comb_buf[2], in_rows, 1, 0).T.astype(BF16)
+    pairs = ((out_ref, out_hbm), (tgrad_ref, tgrad_hbm), (gin_ref, gin_hbm), (gout_ref, gout_hbm))
+    stores = [pltpu.make_async_copy(a, b, store_sem.at[i]) for i, (a, b) in enumerate(pairs)]
+    stores[2].start()
+    stores[3].start()
+
+    for k in range(CHUNKS):
+        first = 1 if k == 0 else 0
+        blocks = ret_recv.at[pl.ds(k * chunk_blocks + first, chunk_blocks - first)]
+        remote(blocks, blocks, ret_send_sem, ret_recv_sem.at[k], sibling).wait_recv()
+        both = ret_recv[pl.ds(k * chunk_blocks, chunk_blocks)].astype(F32)
+        out_rows = both[:, :cap].reshape(chunk_rows, width).astype(BF16)
+        in_rows = both[:, cap:].reshape(chunk_rows, width).astype(BF16)
+        cols = chunk_slice(k)
+        sums = dot(comb_buf[0, :, cols], out_rows, 1, 0)
+        sums = sums + dot(comb_buf[1, :, cols], out_rows, 1, 0)
+        grads = dot(comb_buf[2, :, cols], in_rows, 1, 0)
+        if k > 0:
+            sums, grads = sums_buf[0] + sums, sums_buf[1] + grads
+        if k < CHUNKS - 1:
+            sums_buf[0] = sums
+            sums_buf[1] = grads
+        else:
+            out_ref[...] = sums.T.astype(BF16)
+            tgrad_ref[...] = grads.T.astype(BF16)
+
+    stores[0].start()
+    stores[1].start()
 
     blocks = send_buf.at[pl.ds(0, experts - 1)]
     remote(blocks, blocks, a2a_send_sem, a2a_recv_sem.at[0], sibling).wait_send()
     blocks = ret_send.at[pl.ds(1, experts - 1)]
-    remote(blocks, blocks, ret_send_sem, ret_recv_sem, sibling).wait_send()
+    remote(blocks, blocks, ret_send_sem, ret_recv_sem.at[0], sibling).wait_send()
     for k in range(CHUNKS):
         pair_copy(k).wait_send()
         for n in range(far + near):
@@ -338,18 +406,22 @@
             ag_copy(k, n).wait_send()
         for n in range(zs):
             sib_copy(k, 0, n).wait_send()
+    for store in stores:
+        store.wait()
 
 
 def on_device(tokens, cotangent, w_in, w_out, route_token, route_count, copy_plan, route_prob):
     experts, cap = route_token.shape[1:]
     zs = lax.axis_size("dp") // 2
+    nx = math.isqrt(experts)
+    ny = experts // nx
     count, width = tokens.shape
     hidden = w_in.shape[2]
     half = hidden // 2
     slots = experts * cap
     chunk_rows = slots // CHUNKS
     own_rows = chunk_rows // zs
-    vmem = pl.BlockSpec(memory_space=pltpu.VMEM)
+    hbm = pl.BlockSpec(memory_space=pltpu.HBM)
     dma = pltpu.SemaphoreType.DMA
     out, tgrad, gin, gout = pl.pallas_call(
         functools.partial(moe_kernel, experts, zs),
@@ -359,9 +431,18 @@
             jax.ShapeDtypeStruct((width, hidden), BF16),
             jax.ShapeDtypeStruct((width, hidden), BF16),
         ),
-        in_specs=[vmem] * 8,
-        out_specs=(vmem,) * 4,
+        in_specs=[hbm] * 9,
+        out_specs=(hbm,) * 4,
         scratch_shapes=[
+            pltpu.VMEM((width, count), BF16),
+            pltpu.VMEM((width, count), BF16),
+            pltpu.VMEM((width, hidden), BF16),
+            pltpu.VMEM((width, hidden), BF16),
+            pltpu.VMEM((cap, experts), jnp.int32),
+            pltpu.VMEM((1, experts), jnp.int32),
+            pltpu.VMEM((1, experts), jnp.int32),
+            pltpu.VMEM((cap, experts), F32),
+            pltpu.VMEM((2, experts), jnp.int32),
             pltpu.VMEM((experts, 2 * cap, width), BF16),
             pltpu.VMEM((experts, 2 * cap, width), BF16),
             pltpu.VMEM((slots, width), BF16),
@@ -375,6 +456,13 @@
             pltpu.VMEM((experts, 2 * cap, width), BF16),
             pltpu.VMEM((experts, 2 * cap, width), BF16),
             pltpu.VMEM((3, count, slots), BF16),
+            pltpu.VMEM((2, count, width), F32),
+            pltpu.VMEM((width, count), BF16),
+            pltpu.VMEM((width, count), BF16),
+            pltpu.VMEM((width, hidden), BF16),
+            pltpu.VMEM((width, hidden), BF16),
+            dma((9,)),
+            dma((4,)),
             dma,
             dma((CHUNKS,)),
             dma((CHUNKS,)),
@@ -386,10 +474,10 @@
             dma((CHUNKS, zs)),
             dma((CHUNKS,)),
             dma,
-            dma,
+            dma((CHUNKS,)),
         ],
         compiler_params=pltpu.CompilerParams(
-            collective_id=0, has_side_effects=True, vmem_limit_bytes=40 << 20
+            collective_id=0, has_side_effects=True, vmem_limit_bytes=60 << 20
         ),
         name="moe_layer",
     )(
@@ -401,6 +489,7 @@
         route_count,
         copy_plan[None],
         route_prob[0].T,
+        jnp.asarray(offsets(ny, nx), jnp.int32).T,
     )
     return out.T, tgrad.T, gin[None], gout.T[None]
 

time: 96.3 us -> 90 us (0.935)
  Pallas kernels: 88.1 us -> 84.4 us
  local copies, waits for them, and re-layouts: 7.13 us -> 4.73 us
    pallas_call x1, Pallas kernels: 88.1 us -> 84.4 us  [on_device(): pl.pallas_call(functools.partial(moe_kernel, experts, zs), out_shape=(jax...]
    unnamed x20 -> x8, local copies, waits for them, and re-layouts: 7.13 us -> 4.73 us
where the time goes in v2:
time: 90 us; the launch traced here: 89.8 us
  Pallas kernels  84.4 us (94%)
  local copies, waits for them, and re-layouts  4.73 us (5%)
    pallas_call x1, Pallas kernels, on_device(): pl.pallas_call(functools.partial(moe_kernel, experts, zs), out_shape=(jax...  84.4 us
    unnamed x8, local copies, waits for them, and re-layouts  4.73 us

profile of v2, /device:TPU:1, one launch (start us, length us, event | category | flops | bytes accessed | tf_op | source)
XLA Modules:
  0.0 89.8 jit_solution(17786326570346090392)
XLA Ops:
  0.6 84.4 %moe_layer.1 = (bf16[224,128]{1,0:T(8,128)(2,1)}, bf16[224,128]{1,0:T(8,128)(2,1)}, bf16[224,1024]{1,0:T(8,128)(2,1)}, bf16[224,1024]{1,0:T(8,128)(2,1)}) custom-call(bf16[224,128]{1,0:T(8,128)(2,1)} %bitcast.25, bf16[224,128]{1,0:T(8,128)(2,1)} %bitcast.26, bf16[224,1024]{1,0:T(8,128)(2,1)} %bitcast.21, bf16[224,1024]{1,0:T(8,128)(2,1)} %bitcast.22, ...), custom_call_target="tpu_custom_call" | custom-call | tf_op jit(solution)/shard_map/moe_layer/pallas_call | solution.py:426
  85.0 0.0 copy-start.1
  85.0 1.5 %copy.17 = bf16[128,224]{0,1:T(8,128)(2,1)} copy(bf16[128,224]{0,1:T(8,128)(2,1)} %bitcast.24) | data formatting | bytes 114688
  86.5 0.0 copy-done.1
  86.5 0.6 copy.18
  87.1 0.0 copy-start
  87.1 1.9 %copy.19 = bf16[1,224,1024]{2,1,0:T(8,128)(2,1)} copy(bf16[1,224,1024]{2,1,0:T(8,128)(2,1)} %bitcast.20) | data formatting | bytes 917504
  89.0 0.0 copy-done
  89.0 0.8 copy.20
Async XLA Ops:
  85.0 1.5 %copy-start.1 = (bf16[224,128]{1,0:T(8,128)(2,1)S(1)}, bf16[224,128]{1,0:T(8,128)(2,1)}, u32[]{:S(2)}) copy-start(bf16[224,128]{1,0:T(8,128)(2,1)} %get-tuple-element.9) | copy-start | bytes 172036
  87.1 1.9 %copy-start = (bf16[224,1024]{1,0:T(8,128)(2,1)S(1)}, bf16[224,1024]{1,0:T(8,128)(2,1)}, u32[]{:S(2)}) copy-start(bf16[224,1024]{1,0:T(8,128)(2,1)} %get-tuple-element.11) | copy-start | bytes 1376260

commit v3 on v2

--- a/solution.py
+++ b/solution.py
@@ -47,10 +47,8 @@
     plan_hbm,
     prob_hbm,
     offset_hbm,
-    out_hbm,
-    tgrad_hbm,
-    gin_hbm,
-    gout_hbm,
+    token_hbm,
+    weight_hbm,
     tok_ref,
     cot_ref,
     w_in_ref,
@@ -74,10 +72,8 @@
     ret_recv,
     comb_buf,
     sums_buf,
-    out_ref,
-    tgrad_ref,
-    gin_ref,
-    gout_ref,
+    token_ref,
+    weight_ref,
     load_sem,
     store_sem,
     a2a_send_sem,
@@ -364,13 +360,12 @@
 
     for h in range(2):
         cols = pl.ds(h * half, half)
-        gin_ref[:, cols] = dot(rows_buf[...], act_buf[h, 1], 0, 0).astype(BF16)
-        gout_ref[:, cols] = dot(scaled_buf[...], act_buf[h, 0], 0, 0).astype(BF16)
-
-    pairs = ((out_ref, out_hbm), (tgrad_ref, tgrad_hbm), (gin_ref, gin_hbm), (gout_ref, gout_hbm))
+        weight_ref[0, :, cols] = dot(rows_buf[...], act_buf[h, 1], 0, 0)
+        weight_ref[1, :, cols] = dot(scaled_buf[...], act_buf[h, 0], 0, 0)
+
+    pairs = ((token_ref, token_hbm), (weight_ref, weight_hbm))
     stores = [pltpu.make_async_copy(a, b, store_sem.at[i]) for i, (a, b) in enumerate(pairs)]
-    stores[2].start()
-    stores[3].start()
+    stores[1].start()
 
     for k in range(CHUNKS):
         first = 1 if k == 0 else 0
@@ -389,11 +384,10 @@
             sums_buf[0] = sums
             sums_buf[1] = grads
         else:
-            out_ref[...] = sums.T.astype(BF16)
-            tgrad_ref[...] = grads.T.astype(BF16)
+            token_ref[0] = sums.T
+            token_ref[1] = grads.T
 
     stores[0].start()
-    stores[1].start()
 
     blocks = send_buf.at[pl.ds(0, experts - 1)]
     remote(blocks, blocks, a2a_send_sem, a2a_recv_sem.at[0], sibling).wait_send()
@@ -423,16 +417,14 @@
     own_rows = chunk_rows // zs
     hbm = pl.BlockSpec(memory_space=pltpu.HBM)
     dma = pltpu.SemaphoreType.DMA
-    out, tgrad, gin, gout = pl.pallas_call(
+    token_sums, weight_sums = pl.pallas_call(
         functools.partial(moe_kernel, experts, zs),
         out_shape=(
-            jax.ShapeDtypeStruct((width, count), BF16),
-            jax.ShapeDtypeStruct((width, count), BF16),
-            jax.ShapeDtypeStruct((width, hidden), BF16),
-            jax.ShapeDtypeStruct((width, hidden), BF16),
+            jax.ShapeDtypeStruct((2, width, count), F32),
+            jax.ShapeDtypeStruct((2, width, hidden), F32),
         ),
         in_specs=[hbm] * 9,
-        out_specs=(hbm,) * 4,
+        out_specs=(hbm,) * 2,
         scratch_shapes=[
             pltpu.VMEM((width, count), BF16),
             pltpu.VMEM((width, count), BF16),
@@ -457,12 +449,10 @@
             pltpu.VMEM((experts, 2 * cap, width), BF16),
             pltpu.VMEM((3, count, slots), BF16),
             pltpu.VMEM((2, count, width), F32),
-            pltpu.VMEM((width, count), BF16),
-            pltpu.VMEM((width, count), BF16),
-            pltpu.VMEM((width, hidden), BF16),
-            pltpu.VMEM((width, hidden), BF16),
+            pltpu.VMEM((2, width, count), F32),
+            pltpu.VMEM((2, width, hidden), F32),
             dma((9,)),
-            dma((4,)),
+            dma((2,)),
             dma,
             dma((CHUNKS,)),
             dma((CHUNKS,)),
@@ -491,6 +481,8 @@
         route_prob[0].T,
         jnp.asarray(offsets(ny, nx), jnp.int32).T,
     )
+    out, tgrad = token_sums.astype(BF16)
+    gin, gout = weight_sums.astype(BF16)
     return out.T, tgrad.T, gin[None], gout.T[None]
 
 

time: 90 us -> 89.6 us (level)
  local copies, waits for them, and re-layouts: 4.73 us -> 1.63 us
  other arithmetic: 0 us -> 2.58 us
    unnamed x8 -> x0, local copies, waits for them, and re-layouts: 4.73 us -> none
    convert_element_type x0 -> x2, other arithmetic: none -> 2.58 us  [the longest x1 1.63 us: on_device(): gin, gout = weight_sums.astype(BF16)]
    broadcast_in_dim x0 -> x1, local copies, waits for them, and re-layouts: none -> 0.98 us  [on_device(): return (out.T, tgrad.T, gin[None], gout.T[None])]
where the time goes in v3:
time: 89.6 us; the launch traced here: 89.3 us
  Pallas kernels  84.5 us (94%)
  other arithmetic  2.58 us (3%)
  local copies, waits for them, and re-layouts  1.63 us (2%)
    pallas_call x1, Pallas kernels, on_device(): pl.pallas_call(functools.partial(moe_kernel, experts, zs), out_shape=(jax...  84.5 us

profile of v3, /device:TPU:1, one launch (start us, length us, event | category | flops | bytes accessed | tf_op | source)
XLA Modules:
  0.0 89.3 jit_solution(14699756124806519060)
XLA Ops:
  0.6 84.5 %moe_layer.1 = (f32[2,224,128]{2,1,0:T(8,128)}, f32[2,224,1024]{2,1,0:T(8,128)}) custom-call(bf16[224,128]{1,0:T(8,128)(2,1)} %bitcast.29, bf16[224,128]{1,0:T(8,128)(2,1)} %bitcast.30, bf16[224,1024]{1,0:T(8,128)(2,1)} %bitcast.27, bf16[224,1024]{1,0:T(8,128)(2,1)} %bitcast.28, s32[8,64]{1,0:T(8,128)} %bitcast.31, s32[1,64]{1,0:T(1,128)} %count_hbm.1, ...), custom_call_target="tpu_custom_call" | custom-call | tf_op jit(solution)/shard_map/moe_layer/pallas_call | solution.py:420
  85.1 1.0 %convert_element_type.6 = bf16[2,224,128]{2,1,0:T(8,128)(2,1)S(1)} convert(f32[2,224,128]{2,1,0:T(8,128)} %get-tuple-element.6) | non-fusion elementwise | flops 57344 | bytes 344064 | tf_op jit(solution)/shard_map/convert_element_type | solution.py:484
  86.1 0.6 slice_bitcast_fusion.1
  86.7 1.6 %convert_element_type.7 = bf16[2,224,1024]{2,1,0:T(8,128)(2,1)S(1)} convert(f32[2,224,1024]{2,1,0:T(8,128)} %get-tuple-element.7) | non-fusion elementwise | flops 458752 | bytes 2752512 | tf_op jit(solution)/shard_map/convert_element_type | solution.py:485
  88.4 1.0 %slice_bitcast_fusion = (bf16[1,1024,224]{1,2,0:T(8,128)(2,1)}, bf16[1,224,1024]{2,1,0:T(8,128)(2,1)}) fusion(bf16[2,224,1024]{2,1,0:T(8,128)(2,1)S(1)} %convert_element_type.7), kind=kLoop, calls=%fused_computation | loop fusion | bytes 1835008 | tf_op jit(solution)/shard_map/broadcast_in_dim | solution.py:486
